TPU v7x, 512 devices: a whole 4x4x16 slice. The times are simulated.
512 devices in a mesh: seq: 64 (over z, x), head: 8 (over y, core).
Axes of the slice: x: 4, y: 4, z: 16, core: 2. Of those that a mesh axis runs over, the one named last changes fastest.
Arguments:
- queries: bfloat16 [32768, 3072], P(('seq', 'head')), may hold values from -48 to 48
- keys: bfloat16 [32768, 3072], P(('seq', 'head')), may hold values from -48 to 48
- values: bfloat16 [32768, 3072], P(('seq', 'head')), may hold values from -6 to 6
- tile_mask: int32 [256, 256], P('seq'), may hold values from 0 to 1, as said below
Outputs:
- attended: bfloat16 [32768, 3072], P(('seq', 'head'))
Inputs may be any that keep to these rules, and one draw needn't show every extreme that they name: `tile_mask`: A query tile keeps only key tiles whose column, row and frame-tile each differ from its own by at most one; it always keeps its own tile, and the one tile whose column, row and frame-tile are all one more than its own (and the one whose three are all one less), where that tile exists.
All inputs are finite; a program needn't handle non-finite values.
Results may differ from a plain program's by a relative error of at most 0.0046.
Values may be sent and summed in bfloat16 or wider, within the bound.
A program may use at most 64 MiB of HBM per device.

v0:
```python
import math

import jax
import jax.numpy as jnp
from jax import lax
from jax.sharding import PartitionSpec as P

HEAD_DIM = 128
TILE_H = 4


def shifted(value, axis, steps):
    count = lax.axis_size(axis)
    initial, last = (max(0, -steps), min(count, count - steps))
    return lax.ppermute(value, axis, [(source, source + steps) for source in range(initial, last)])


def body(queries, keys, values, tile_mask):
    q_local, k_local, v_local = (
        lax.all_to_all(queries, "head", split_axis=1, concat_axis=0, tiled=True),
        lax.all_to_all(keys, "head", split_axis=1, concat_axis=0, tiled=True),
        lax.all_to_all(values, "head", split_axis=1, concat_axis=0, tiled=True),
    )
    length = q_local.shape[0]
    tiles_dev = tile_mask.shape[0]
    tile_len = length // tiles_dev
    groups_here = q_local.shape[1] // HEAD_DIM
    position = lax.axis_index("seq")
    shards = lax.axis_size("seq")
    stride = TILE_H
    offsets = [-stride - 1, -stride, -stride + 1, -1, 0, 1, stride - 1, stride, stride + 1]
    key_parts = []
    value_parts = []
    for offset in offsets:
        if offset == 0:
            key_parts.append(k_local)
            value_parts.append(v_local)
        else:
            moved_k, moved_v = shifted((k_local, v_local), "seq", -offset)
            key_parts.append(moved_k)
            value_parts.append(moved_v)
    key_all = jnp.concatenate(key_parts, axis=0)
    value_all = jnp.concatenate(value_parts, axis=0)
    flag_parts = []
    for offset in offsets:
        target = position + offset
        begin = jnp.clip(target, 0, shards - 1) * tiles_dev
        piece = lax.dynamic_slice_in_dim(tile_mask, begin, tiles_dev, 1)
        inside = ((target >= 0) & (target < shards)).astype(jnp.int32)
        flag_parts.append(piece * inside)
    near_flags = jnp.concatenate(flag_parts, axis=1) > 0
    keys_count = key_all.shape[0]
    block_rows = min(512, length)
    blocks = length // block_rows
    tiles_block = block_rows // tile_len
    scale = 1.0 / math.sqrt(HEAD_DIM)

    def one_block(index):
        head = index // blocks
        part_index = index % blocks
        query_block = lax.dynamic_slice(
            q_local, (part_index * block_rows, head * HEAD_DIM), (block_rows, HEAD_DIM)
        )
        key_head = lax.dynamic_slice_in_dim(key_all, head * HEAD_DIM, HEAD_DIM, 1)
        value_head = lax.dynamic_slice_in_dim(value_all, head * HEAD_DIM, HEAD_DIM, 1)
        scores = (
            lax.dot_general(
                query_block, key_head, (((1,), (1,)), ((), ())), preferred_element_type=jnp.float32
            )
            * scale
        )
        wide = jnp.broadcast_to(
            near_flags[:, None, :, None], (tiles_block, tile_len, near_flags.shape[1], tile_len)
        )
        wide = wide.reshape(block_rows, keys_count)
        scores = jnp.where(wide, scores, -jnp.inf)
        top = jnp.max(scores, axis=1, keepdims=True)
        weights = jnp.exp(scores - top)
        total = jnp.sum(weights, axis=1, keepdims=True)
        probs = weights.astype(jnp.bfloat16)
        return jnp.dot(probs, value_head, preferred_element_type=jnp.float32) / total

    outputs = lax.map(one_block, jnp.arange(groups_here * blocks, dtype=jnp.int32))
    attended = (
        jnp.transpose(outputs, (1, 0, 2))
        .reshape(length, groups_here * HEAD_DIM)
        .astype(jnp.bfloat16)
    )
    return lax.all_to_all(attended, "head", split_axis=0, concat_axis=1, tiled=True)


def solution(mesh):
    placed = (
        P(("seq", "head"), None),
        P(("seq", "head"), None),
        P(("seq", "head"), None),
        P("seq", None),
    )
    return jax.shard_map(
        body, mesh=mesh, in_specs=placed, out_specs=P(("seq", "head"), None), check_vma=False
    )
```

profile of v0, /device:TPU:70, one launch (start us, length us, event | category | flops | bytes accessed | tf_op | source)
XLA Modules:
  0.0 219.4 jit_solution(1306422877454395606)
XLA Ops:
  1.1 13.3 %all_to_all.73 = bf16[64,8,384]{2,0,1:T(8,128)(2,1)} all-to-all(bf16[64,8,384]{2,0,1:T(8,128)(2,1)S(1)} %bitcast.50), channel_id=1, replica_groups=mesh['seq'=64,'head'=8] {'head'}, dimensions={1} | all-to-all | bytes 786432 | tf_op jit(solution)/shard_map/all_to_all | solution.py:22
  14.4 6.3 %collective-permute-start.8 = (bf16[512,384]{1,0:T(8,128)(2,1)}, bf16[512,384]{1,0:T(8,128)(2,1)S(1)}, u32[]{:S(2)}, u32[]{:S(2)}) collective-permute-start(bf16[512,384]{1,0:T(8,128)(2,1)} %bitcast.8), channel_id=1, source_target_pairs={{0,40},{8,48},{16,56},{24,64},{32,72},{40,80},{48,88},{56,96},{64,... | collective-permute-start | bytes 1179656 | tf_op jit(solution)/shard_map/ppermute | solution.py:15
  20.7 1.8 copy.55
  22.5 4.1 %all-to-all-start.1 = ((bf16[64,8,384]{2,0,1:T(8,128)(2,1)}), bf16[64,8,384]{2,0,1:T(8,128)(2,1)}, u32[]{:S(2)}, u32[]{:S(2)}) async-start(bf16[64,8,384]{2,0,1:T(8,128)(2,1)} %bitcast.37), calls=%async_computation.1 | async-start | bytes 786432 | tf_op jit(solution)/shard_map/all_to_all | solution.py:21
  26.6 3.8 %collective-permute-start.9 = (bf16[512,384]{1,0:T(8,128)(2,1)}, bf16[512,384]{1,0:T(8,128)(2,1)S(1)}, u32[]{:S(2)}, u32[]{:S(2)}) collective-permute-start(bf16[512,384]{1,0:T(8,128)(2,1)} %bitcast.8), channel_id=1, source_target_pairs={{0,32},{8,40},{16,48},{24,56},{32,64},{40,72},{48,80},{56,88},{64,... | collective-permute-start | bytes 1179656 | tf_op jit(solution)/shard_map/ppermute | solution.py:15
  31.7 3.4 %collective-permute-start.10 = (bf16[512,384]{1,0:T(8,128)(2,1)}, bf16[512,384]{1,0:T(8,128)(2,1)S(1)}, u32[]{:S(2)}, u32[]{:S(2)}) collective-permute-start(bf16[512,384]{1,0:T(8,128)(2,1)} %bitcast.8), channel_id=1, source_target_pairs={{0,24},{8,32},{16,40},{24,48},{32,56},{40,64},{48,72},{56,80},{64,... | collective-permute-start | bytes 1179656 | tf_op jit(solution)/shard_map/ppermute | solution.py:15
  35.1 5.0 %collective-permute-start.11 = (bf16[512,384]{1,0:T(8,128)(2,1)}, bf16[512,384]{1,0:T(8,128)(2,1)S(1)}, u32[]{:S(2)}, u32[]{:S(2)}) collective-permute-start(bf16[512,384]{1,0:T(8,128)(2,1)} %bitcast.8), channel_id=1, source_target_pairs={{0,8},{8,16},{16,24},{24,32},{32,40},{40,48},{48,56},{56,64},{64,7... | collective-permute-start | bytes 1179656 | tf_op jit(solution)/shard_map/ppermute | solution.py:15
  41.0 1.9 collective-permute-start.12
  43.0 4.6 %all-to-all-start = ((bf16[64,8,384]{2,0,1:T(8,128)(2,1)}), bf16[64,8,384]{2,0,1:T(8,128)(2,1)}, u32[]{:S(2)}, u32[]{:S(2)}) async-start(bf16[64,8,384]{2,0,1:T(8,128)(2,1)} %bitcast.38), calls=%async_computation | async-start | bytes 786432 | tf_op jit(solution)/shard_map/all_to_all | solution.py:20
  47.6 8.6 %collective-permute-start = (bf16[512,384]{1,0:T(8,128)(2,1)}, bf16[512,384]{1,0:T(8,128)(2,1)S(1)}, u32[]{:S(2)}, u32[]{:S(2)}) collective-permute-start(bf16[512,384]{1,0:T(8,128)(2,1)} %bitcast.5), channel_id=1, source_target_pairs={{0,40},{8,48},{16,56},{24,64},{32,72},{40,80},{48,88},{56,96},{64,... | collective-permute-start | bytes 1179656 | tf_op jit(solution)/shard_map/ppermute | solution.py:15
  56.3 3.8 %collective-permute-start.1 = (bf16[512,384]{1,0:T(8,128)(2,1)}, bf16[512,384]{1,0:T(8,128)(2,1)S(1)}, u32[]{:S(2)}, u32[]{:S(2)}) collective-permute-start(bf16[512,384]{1,0:T(8,128)(2,1)} %bitcast.5), channel_id=1, source_target_pairs={{0,32},{8,40},{16,48},{24,56},{32,64},{40,72},{48,80},{56,88},{64,... | collective-permute-start | bytes 1179656 | tf_op jit(solution)/shard_map/ppermute | solution.py:15
  60.2 1.9 collective-permute-start.2
  62.2 2.1 collective-permute-done.11
  64.3 6.4 %collective-permute-start.3 = (bf16[512,384]{1,0:T(8,128)(2,1)}, bf16[512,384]{1,0:T(8,128)(2,1)S(1)}, u32[]{:S(2)}, u32[]{:S(2)}) collective-permute-start(bf16[512,384]{1,0:T(8,128)(2,1)} %bitcast.5), channel_id=1, source_target_pairs={{0,8},{8,16},{16,24},{24,32},{32,40},{40,48},{48,56},{56,64},{64,7... | collective-permute-start | bytes 1179656 | tf_op jit(solution)/shard_map/ppermute | solution.py:15
  71.8 9.4 %collective-permute-done = bf16[512,384]{1,0:T(8,128)(2,1)S(1)} collective-permute-done((bf16[512,384]{1,0:T(8,128)(2,1)}, bf16[512,384]{1,0:T(8,128)(2,1)S(1)}, u32[]{:S(2)}, u32[]{:S(2)}) %collective-permute-start) | collective-permute-done | bytes 393248 | tf_op jit(solution)/shard_map/ppermute | solution.py:15
  81.2 1.9 collective-permute-start.13
  83.1 6.5 %collective-permute-done.1 = bf16[512,384]{1,0:T(8,128)(2,1)S(1)} collective-permute-done((bf16[512,384]{1,0:T(8,128)(2,1)}, bf16[512,384]{1,0:T(8,128)(2,1)S(1)}, u32[]{:S(2)}, u32[]{:S(2)}) %collective-permute-start.1) | collective-permute-done | bytes 393248 | tf_op jit(solution)/shard_map/ppermute | solution.py:15
  89.6 1.9 collective-permute-start.14
  91.6 6.4 %collective-permute-done.2 = bf16[512,384]{1,0:T(8,128)(2,1)S(1)} collective-permute-done((bf16[512,384]{1,0:T(8,128)(2,1)}, bf16[512,384]{1,0:T(8,128)(2,1)S(1)}, u32[]{:S(2)}, u32[]{:S(2)}) %collective-permute-start.2) | collective-permute-done | bytes 393248 | tf_op jit(solution)/shard_map/ppermute | solution.py:15
  98.0 1.9 collective-permute-start.15
  100.0 5.1 %collective-permute-done.3 = bf16[512,384]{1,0:T(8,128)(2,1)S(1)} collective-permute-done((bf16[512,384]{1,0:T(8,128)(2,1)}, bf16[512,384]{1,0:T(8,128)(2,1)S(1)}, u32[]{:S(2)}, u32[]{:S(2)}) %collective-permute-start.3) | collective-permute-done | bytes 393248 | tf_op jit(solution)/shard_map/ppermute | solution.py:15
  105.1 1.9 collective-permute-start.4
  108.1 3.5 %collective-permute-start.5 = (bf16[512,384]{1,0:T(8,128)(2,1)}, bf16[512,384]{1,0:T(8,128)(2,1)S(1)}, u32[]{:S(2)}, u32[]{:S(2)}) collective-permute-start(bf16[512,384]{1,0:T(8,128)(2,1)} %bitcast.5), channel_id=1, source_target_pairs={{24,0},{32,8},{40,16},{48,24},{56,32},{64,40},{72,48},{80,56},{88,... | collective-permute-start | bytes 1179656 | tf_op jit(solution)/shard_map/ppermute | solution.py:15
  112.7 1.9 collective-permute-start.6
  114.7 2.1 collective-permute-start.7
  116.9 7.6 %collective-permute-done.15 = bf16[512,384]{1,0:T(8,128)(2,1)S(1)} collective-permute-done((bf16[512,384]{1,0:T(8,128)(2,1)}, bf16[512,384]{1,0:T(8,128)(2,1)S(1)}, u32[]{:S(2)}, u32[]{:S(2)}) %collective-permute-start.15) | collective-permute-done | bytes 393248 | tf_op jit(solution)/shard_map/ppermute | solution.py:15
  124.6 3.4 %collective-permute-done.4 = bf16[512,384]{1,0:T(8,128)(2,1)S(1)} collective-permute-done((bf16[512,384]{1,0:T(8,128)(2,1)}, bf16[512,384]{1,0:T(8,128)(2,1)S(1)}, u32[]{:S(2)}, u32[]{:S(2)}) %collective-permute-start.4) | collective-permute-done | bytes 393248 | tf_op jit(solution)/shard_map/ppermute | solution.py:15
  128.4 35.5 %collective-permute-done.7 = bf16[512,384]{1,0:T(8,128)(2,1)S(1)} collective-permute-done((bf16[512,384]{1,0:T(8,128)(2,1)}, bf16[512,384]{1,0:T(8,128)(2,1)S(1)}, u32[]{:S(2)}, u32[]{:S(2)}) %collective-permute-start.7) | collective-permute-done | bytes 393248 | tf_op jit(solution)/shard_map/ppermute | solution.py:15
  164.0 41.6 %while.12 = (s32[]{:T(128)}, bf16[3,512,128]{2,1,0:T(8,128)(2,1)}, pred[4,36]{0,1:T(8,128)(4,1)S(1)}, s32[3]{0:T(128)S(1)}, bf16[512,384]{1,0:T(8,128)(2,1)}, /*...) while((s32[]{:T(128)}, bf16[3,512,128]{2,1,0:T(8,128)(2,1)}, ...), condition=%wide.region_3.4_spmd, body=%wide.region_0.3_spmd.sunk | while | flops 1224539136 | bytes 45231932 | solution.py:83
  165.2 1.3 broadcast_in_dim.31
  166.5 1.1 copy.59
  167.6 2.5 %copy.60 = pred[512,4608]{1,0:T(32,128)(4,1)S(1)} copy(pred[512,4608]{0,1:T(8,128)(4,1)S(1)} %bitcast.47) | data formatting | bytes 4718592 | tf_op jit(solution)/shard_map/while/body/eval_jaxpr/reshape | solution.py:75
  170.1 3.0 %fusion.42 = (f32[512]{0:T(512)S(1)}, f32[512,4608]{1,0:T(8,128)S(1)}) fusion(pred[512,4608]{1,0:T(32,128)(4,1)S(1)} %copy.60, bf16[4608,384]{1,0:T(8,128)(2,1)S(1)} %get-tuple-element.203, s32[]{:T(128)S(6)} %select_n.64, bf16[512,384]{1,0:T(8,128)(2,1)} %get-tuple-element.202), kind=kOutput, calls=%fused_computation.56.clone.1 | convolution fusion | flops 611057152 | bytes 13110272 | tf_op jit(solution)/shard_map/while/body/eval_jaxpr/dot_general | solution.py:67
  173.1 1.4 fusion.43
  174.5 3.4 %fusion.44 = bf16[3,512,128]{2,1,0:T(8,128)(2,1)} fusion(bf16[3,512,128]{2,1,0:T(8,128)(2,1)} %get-tuple-element.188, s32[]{:T(128)} %get-tuple-element.187, bf16[4608,384]{1,0:T(8,128)(2,1)} %get-tuple-element.204, s32[]{:T(128)S(6)} %select_n.64, f32[512,4608]{1,0:T(8,128)S(1)} %get-tuple-element.174, f32[512]{0:T(512)S(1)} %get-tuple-element.175, ...), kind=kOutput, calls=%fused_computation.11.clone.1 | convolution fusion | flops 608763904 | bytes 10883588 | tf_op jit(solution)/shard_map/while/body/eval_jaxpr/dot_general | solution.py:81
  179.0 1.3 broadcast_in_dim.31
  180.3 1.1 copy.59
  181.5 2.5 %copy.60 = pred[512,4608]{1,0:T(32,128)(4,1)S(1)} copy(pred[512,4608]{0,1:T(8,128)(4,1)S(1)} %bitcast.47) | data formatting | bytes 4718592 | tf_op jit(solution)/shard_map/while/body/eval_jaxpr/reshape | solution.py:75
  184.0 3.0 %fusion.42 = (f32[512]{0:T(512)S(1)}, f32[512,4608]{1,0:T(8,128)S(1)}) fusion(pred[512,4608]{1,0:T(32,128)(4,1)S(1)} %copy.60, bf16[4608,384]{1,0:T(8,128)(2,1)S(1)} %get-tuple-element.203, s32[]{:T(128)S(6)} %select_n.64, bf16[512,384]{1,0:T(8,128)(2,1)} %get-tuple-element.202), kind=kOutput, calls=%fused_computation.56.clone.1 | convolution fusion | flops 611057152 | bytes 13110272 | tf_op jit(solution)/shard_map/while/body/eval_jaxpr/dot_general | solution.py:67
  186.9 1.4 fusion.43
  188.4 3.4 %fusion.44 = bf16[3,512,128]{2,1,0:T(8,128)(2,1)} fusion(bf16[3,512,128]{2,1,0:T(8,128)(2,1)} %get-tuple-element.188, s32[]{:T(128)} %get-tuple-element.187, bf16[4608,384]{1,0:T(8,128)(2,1)} %get-tuple-element.204, s32[]{:T(128)S(6)} %select_n.64, f32[512,4608]{1,0:T(8,128)S(1)} %get-tuple-element.174, f32[512]{0:T(512)S(1)} %get-tuple-element.175, ...), kind=kOutput, calls=%fused_computation.11.clone.1 | convolution fusion | flops 608763904 | bytes 10883588 | tf_op jit(solution)/shard_map/while/body/eval_jaxpr/dot_general | solution.py:81
  192.9 1.3 broadcast_in_dim.31
  195.3 2.5 %copy.60 = pred[512,4608]{1,0:T(32,128)(4,1)S(1)} copy(pred[512,4608]{0,1:T(8,128)(4,1)S(1)} %bitcast.47) | data formatting | bytes 4718592 | tf_op jit(solution)/shard_map/while/body/eval_jaxpr/reshape | solution.py:75
  197.8 3.0 %fusion.42 = (f32[512]{0:T(512)S(1)}, f32[512,4608]{1,0:T(8,128)S(1)}) fusion(pred[512,4608]{1,0:T(32,128)(4,1)S(1)} %copy.60, bf16[4608,384]{1,0:T(8,128)(2,1)S(1)} %get-tuple-element.203, s32[]{:T(128)S(6)} %select_n.64, bf16[512,384]{1,0:T(8,128)(2,1)} %get-tuple-element.202), kind=kOutput, calls=%fused_computation.56.clone.1 | convolution fusion | flops 611057152 | bytes 13110272 | tf_op jit(solution)/shard_map/while/body/eval_jaxpr/dot_general | solution.py:67
  200.8 1.4 fusion.43
  202.2 3.4 %fusion.44 = bf16[3,512,128]{2,1,0:T(8,128)(2,1)} fusion(bf16[3,512,128]{2,1,0:T(8,128)(2,1)} %get-tuple-element.188, s32[]{:T(128)} %get-tuple-element.187, bf16[4608,384]{1,0:T(8,128)(2,1)} %get-tuple-element.204, s32[]{:T(128)S(6)} %select_n.64, f32[512,4608]{1,0:T(8,128)S(1)} %get-tuple-element.174, f32[512]{0:T(512)S(1)} %get-tuple-element.175, ...), kind=kOutput, calls=%fused_computation.11.clone.1 | convolution fusion | flops 608763904 | bytes 10883588 | tf_op jit(solution)/shard_map/while/body/eval_jaxpr/dot_general | solution.py:81
  205.6 1.3 copy.42
  207.3 11.3 %all_to_all.74 = bf16[8,64,384]{2,1,0:T(8,128)(2,1)S(1)} all-to-all(bf16[8,64,384]{2,1,0:T(8,128)(2,1)S(1)} %convert_element_type.54), channel_id=1, replica_groups=mesh['seq'=64,'head'=8] {'head'}, dimensions={0} | all-to-all | bytes 786432 | tf_op jit(solution)/shard_map/all_to_all | solution.py:89
  (46 shorter events, 11.5 us)
Async XLA Ops:
  0.0 40.2 %copy-start.1 = (bf16[64,3072]{1,0:T(8,128)(2,1)S(1)}, bf16[64,3072]{1,0:T(8,128)(2,1)}, u32[]{:S(2)}) copy-start(bf16[64,3072]{1,0:T(8,128)(2,1)} %param.6) | copy-start | bytes 1179652
  14.4 33.2 %collective-permute-start.8 = (bf16[512,384]{1,0:T(8,128)(2,1)}, bf16[512,384]{1,0:T(8,128)(2,1)S(1)}, u32[]{:S(2)}, u32[]{:S(2)}) collective-permute-start(bf16[512,384]{1,0:T(8,128)(2,1)} %bitcast.8), channel_id=1, source_target_pairs={{0,40},{8,48},{16,56},{24,64},{32,72},{40,80},{48,88},{56,96},{64,... | collective-permute-start | bytes 1179656 | tf_op jit(solution)/shard_map/ppermute | solution.py:15
  22.5 20.5 %all-to-all-start.1 = ((bf16[64,8,384]{2,0,1:T(8,128)(2,1)}), bf16[64,8,384]{2,0,1:T(8,128)(2,1)}, u32[]{:S(2)}, u32[]{:S(2)}) async-start(bf16[64,8,384]{2,0,1:T(8,128)(2,1)} %bitcast.37), calls=%async_computation.1 | async-start | bytes 786432 | tf_op jit(solution)/shard_map/all_to_all | solution.py:21
  26.6 29.6 %collective-permute-start.9 = (bf16[512,384]{1,0:T(8,128)(2,1)}, bf16[512,384]{1,0:T(8,128)(2,1)S(1)}, u32[]{:S(2)}, u32[]{:S(2)}) collective-permute-start(bf16[512,384]{1,0:T(8,128)(2,1)} %bitcast.8), channel_id=1, source_target_pairs={{0,32},{8,40},{16,48},{24,56},{32,64},{40,72},{48,80},{56,88},{64,... | collective-permute-start | bytes 1179656 | tf_op jit(solution)/shard_map/ppermute | solution.py:15
  31.7 28.5 %collective-permute-start.10 = (bf16[512,384]{1,0:T(8,128)(2,1)}, bf16[512,384]{1,0:T(8,128)(2,1)S(1)}, u32[]{:S(2)}, u32[]{:S(2)}) collective-permute-start(bf16[512,384]{1,0:T(8,128)(2,1)} %bitcast.8), channel_id=1, source_target_pairs={{0,24},{8,32},{16,40},{24,48},{32,56},{40,64},{48,72},{56,80},{64,... | collective-permute-start | bytes 1179656 | tf_op jit(solution)/shard_map/ppermute | solution.py:15
  35.1 29.1 %collective-permute-start.11 = (bf16[512,384]{1,0:T(8,128)(2,1)}, bf16[512,384]{1,0:T(8,128)(2,1)S(1)}, u32[]{:S(2)}, u32[]{:S(2)}) collective-permute-start(bf16[512,384]{1,0:T(8,128)(2,1)} %bitcast.8), channel_id=1, source_target_pairs={{0,8},{8,16},{16,24},{24,32},{32,40},{40,48},{48,56},{56,64},{64,7... | collective-permute-start | bytes 1179656 | tf_op jit(solution)/shard_map/ppermute | solution.py:15
  41.0 67.1 %collective-permute-start.12 = (bf16[512,384]{1,0:T(8,128)(2,1)}, bf16[512,384]{1,0:T(8,128)(2,1)}, u32[]{:S(2)}, u32[]{:S(2)}) collective-permute-start(bf16[512,384]{1,0:T(8,128)(2,1)} %bitcast.8), channel_id=1, source_target_pairs={{8,0},{16,8},{24,16},{32,24},{40,32},{48,40},{56,48},{64,56},{72,6... | collective-permute-start | bytes 1179656 | tf_op jit(solution)/shard_map/ppermute | solution.py:15
  43.0 121.0 %all-to-all-start = ((bf16[64,8,384]{2,0,1:T(8,128)(2,1)}), bf16[64,8,384]{2,0,1:T(8,128)(2,1)}, u32[]{:S(2)}, u32[]{:S(2)}) async-start(bf16[64,8,384]{2,0,1:T(8,128)(2,1)} %bitcast.38), calls=%async_computation | async-start | bytes 786432 | tf_op jit(solution)/shard_map/all_to_all | solution.py:20
  47.6 33.5 %collective-permute-start = (bf16[512,384]{1,0:T(8,128)(2,1)}, bf16[512,384]{1,0:T(8,128)(2,1)S(1)}, u32[]{:S(2)}, u32[]{:S(2)}) collective-permute-start(bf16[512,384]{1,0:T(8,128)(2,1)} %bitcast.5), channel_id=1, source_target_pairs={{0,40},{8,48},{16,56},{24,64},{32,72},{40,80},{48,88},{56,96},{64,... | collective-permute-start | bytes 1179656 | tf_op jit(solution)/shard_map/ppermute | solution.py:15
  56.3 33.3 %collective-permute-start.1 = (bf16[512,384]{1,0:T(8,128)(2,1)}, bf16[512,384]{1,0:T(8,128)(2,1)S(1)}, u32[]{:S(2)}, u32[]{:S(2)}) collective-permute-start(bf16[512,384]{1,0:T(8,128)(2,1)} %bitcast.5), channel_id=1, source_target_pairs={{0,32},{8,40},{16,48},{24,56},{32,64},{40,72},{48,80},{56,88},{64,... | collective-permute-start | bytes 1179656 | tf_op jit(solution)/shard_map/ppermute | solution.py:15
  60.2 37.8 %collective-permute-start.2 = (bf16[512,384]{1,0:T(8,128)(2,1)}, bf16[512,384]{1,0:T(8,128)(2,1)S(1)}, u32[]{:S(2)}, u32[]{:S(2)}) collective-permute-start(bf16[512,384]{1,0:T(8,128)(2,1)} %bitcast.5), channel_id=1, source_target_pairs={{0,24},{8,32},{16,40},{24,48},{32,56},{40,64},{48,72},{56,80},{64,... | collective-permute-start | bytes 1179656 | tf_op jit(solution)/shard_map/ppermute | solution.py:15
  64.3 40.8 %collective-permute-start.3 = (bf16[512,384]{1,0:T(8,128)(2,1)}, bf16[512,384]{1,0:T(8,128)(2,1)S(1)}, u32[]{:S(2)}, u32[]{:S(2)}) collective-permute-start(bf16[512,384]{1,0:T(8,128)(2,1)} %bitcast.5), channel_id=1, source_target_pairs={{0,8},{8,16},{16,24},{24,32},{32,40},{40,48},{48,56},{56,64},{64,7... | collective-permute-start | bytes 1179656 | tf_op jit(solution)/shard_map/ppermute | solution.py:15
  81.2 31.5 %collective-permute-start.13 = (bf16[512,384]{1,0:T(8,128)(2,1)}, bf16[512,384]{1,0:T(8,128)(2,1)S(1)}, u32[]{:S(2)}, u32[]{:S(2)}) collective-permute-start(bf16[512,384]{1,0:T(8,128)(2,1)} %bitcast.8), channel_id=1, source_target_pairs={{24,0},{32,8},{40,16},{48,24},{56,32},{64,40},{72,48},{80,56},{88,... | collective-permute-start | bytes 1179656 | tf_op jit(solution)/shard_map/ppermute | solution.py:15
  89.6 25.1 %collective-permute-start.14 = (bf16[512,384]{1,0:T(8,128)(2,1)}, bf16[512,384]{1,0:T(8,128)(2,1)S(1)}, u32[]{:S(2)}, u32[]{:S(2)}) collective-permute-start(bf16[512,384]{1,0:T(8,128)(2,1)} %bitcast.8), channel_id=1, source_target_pairs={{32,0},{40,8},{48,16},{56,24},{64,32},{72,40},{80,48},{88,56},{96,... | collective-permute-start | bytes 1179656 | tf_op jit(solution)/shard_map/ppermute | solution.py:15
  98.0 26.5 %collective-permute-start.15 = (bf16[512,384]{1,0:T(8,128)(2,1)}, bf16[512,384]{1,0:T(8,128)(2,1)S(1)}, u32[]{:S(2)}, u32[]{:S(2)}) collective-permute-start(bf16[512,384]{1,0:T(8,128)(2,1)} %bitcast.8), channel_id=1, source_target_pairs={{40,0},{48,8},{56,16},{64,24},{72,32},{80,40},{88,48},{96,56},{104... | collective-permute-start | bytes 1179656 | tf_op jit(solution)/shard_map/ppermute | solution.py:15
  105.1 22.9 %collective-permute-start.4 = (bf16[512,384]{1,0:T(8,128)(2,1)}, bf16[512,384]{1,0:T(8,128)(2,1)S(1)}, u32[]{:S(2)}, u32[]{:S(2)}) collective-permute-start(bf16[512,384]{1,0:T(8,128)(2,1)} %bitcast.5), channel_id=1, source_target_pairs={{8,0},{16,8},{24,16},{32,24},{40,32},{48,40},{56,48},{64,56},{72,6... | collective-permute-start | bytes 1179656 | tf_op jit(solution)/shard_map/ppermute | solution.py:15
  108.1 19.9 %collective-permute-start.5 = (bf16[512,384]{1,0:T(8,128)(2,1)}, bf16[512,384]{1,0:T(8,128)(2,1)S(1)}, u32[]{:S(2)}, u32[]{:S(2)}) collective-permute-start(bf16[512,384]{1,0:T(8,128)(2,1)} %bitcast.5), channel_id=1, source_target_pairs={{24,0},{32,8},{40,16},{48,24},{56,32},{64,40},{72,48},{80,56},{88,... | collective-permute-start | bytes 1179656 | tf_op jit(solution)/shard_map/ppermute | solution.py:15
  112.7 15.6 %collective-permute-start.6 = (bf16[512,384]{1,0:T(8,128)(2,1)}, bf16[512,384]{1,0:T(8,128)(2,1)S(1)}, u32[]{:S(2)}, u32[]{:S(2)}) collective-permute-start(bf16[512,384]{1,0:T(8,128)(2,1)} %bitcast.5), channel_id=1, source_target_pairs={{32,0},{40,8},{48,16},{56,24},{64,32},{72,40},{80,48},{88,56},{96,... | collective-permute-start | bytes 1179656 | tf_op jit(solution)/shard_map/ppermute | solution.py:15
  114.7 49.2 %collective-permute-start.7 = (bf16[512,384]{1,0:T(8,128)(2,1)}, bf16[512,384]{1,0:T(8,128)(2,1)S(1)}, u32[]{:S(2)}, u32[]{:S(2)}) collective-permute-start(bf16[512,384]{1,0:T(8,128)(2,1)} %bitcast.5), channel_id=1, source_target_pairs={{40,0},{48,8},{56,16},{64,24},{72,32},{80,40},{88,48},{96,56},{104... | collective-permute-start | bytes 1179656 | tf_op jit(solution)/shard_map/ppermute | solution.py:15
  124.6 3.8 %copy-start = (bf16[4608,384]{1,0:T(8,128)(2,1)}, bf16[4608,384]{1,0:T(8,128)(2,1)S(1)}, u32[]{:S(2)}) copy-start(bf16[4608,384]{1,0:T(8,128)(2,1)S(1)} %constant_dynamic-update-slice_fusion.9) | copy-start | bytes 10616836
where the time goes:
time: 221 us; the launch traced here: 219 us
  waiting for transfers between devices  76.2 us (34%)
  starting transfers between devices  65 us (29%)
  local copies, waits for them, and re-layouts  26.9 us (12%)
  blocking collectives  24.6 us (11%)
  matrix products  19.1 us (9%)
  other arithmetic  5.35 us (2%)
    ppermute x16, waiting for transfers between devices, shifted(): lax.ppermute(value, axis, [(source, source + steps) for source in range(i...  76.2 us
    ppermute x16, starting transfers between devices, shifted(): lax.ppermute(value, axis, [(source, source + steps) for source in range(i...  56.3 us
    all_to_all x1, blocking collectives, body(): lax.all_to_all(values, 'head', split_axis=1, concat_axis=0, tiled=True)  13.3 us
    all_to_all x1, blocking collectives, body(): lax.all_to_all(attended, 'head', split_axis=0, concat_axis=1, tiled=True)  11.3 us
    dot_general x3, matrix products, one_block(): jnp.dot(probs, value_head, preferred_element_type=jnp.float32) / total  10.1 us
    dot_general x3, matrix products, one_block(): lax.dot_general(query_block, key_head, (((1,), (1,)), ((), ())), preferre...  8.93 us
    reshape x3, local copies, waits for them, and re-layouts, one_block(): wide = wide.reshape(block_rows, keys_count)  7.51 us
    all_to_all x1, starting transfers between devices, body(): lax.all_to_all(queries, 'head', split_axis=1, concat_axis=0, tiled=True)  4.65 us
  transfers between devices with their start and end apart: 18, of which 9 were waited for; matrix products, arithmetic and copies ran while one was open for 4% of the time, Pallas kernels for 0%

commit v1 on v0

v1 whole, which is shorter than its diff:
```python
import math

import jax
import jax.numpy as jnp
from jax import lax
from jax.experimental import pallas as pl
from jax.experimental.pallas import tpu as pltpu
from jax.sharding import PartitionSpec as P

MESH = pl.DeviceIdType.MESH
BF16, F32 = jnp.bfloat16, jnp.float32
FRAMES, ROWS, COLS = 16, 4, 4
TILE, HALF, DIM = 128, 64, 128
GROUPS = 6
MASKED = -1e30


def kernel(q_ref, k_ref, v_ref, mask_ref, out_ref, kv, qb, mb, bias, scores, probs, top, total, acc, ob,
           recv_in, recv_z, recv_x, recv_q, recv_mask, recv_out,
           send_k, send_v, send_q, send_mask, send_z, send_x, send_out):
    seq, head = lax.axis_index("seq"), lax.axis_index("head")
    z, x = seq // ROWS, seq % ROWS
    y, c = head // 2, head % 2
    p, pair = y % 2, 2 * x + y // 2

    barrier = pltpu.get_barrier_semaphore()
    own = x * 8 + head

    def greet(k, carry):
        other = (own + k) % 32
        pl.semaphore_signal(barrier, inc=1, device_id=(z * ROWS + other // 8, other % 8), device_id_type=MESH)
        return carry

    lax.fori_loop(1, 32, greet, 0)
    above = ((z + 1) % FRAMES) * ROWS + x
    below = ((z + FRAMES - 1) % FRAMES) * ROWS + x
    for there in (above, below):
        pl.semaphore_signal(barrier, inc=1, device_id=(there, head), device_id_type=MESH)
    pl.semaphore_wait(barrier, 33)

    row_there = jnp.where(x < 2, x, 3 - x)
    core_there = x // 2
    near = jnp.where(y < 2, y, 3 - y)

    def target(phase, j):
        p_t = (y // 2 + phase) % 2
        x_t = (x + j) % 4
        yh_t = (y // 2 + j // 4) % 2
        y_t = 2 * yh_t + p_t
        w_t = 2 * x_t + yh_t
        col = near if phase == 0 else 3 - near
        here = (x_t == x) & (y_t == y) & (core_there == c)
        return (z * ROWS + x_t, 2 * y_t + core_there), 3 * w_t + 2 * p_t, 3 * w_t + 1, col, here

    def part(ref, h):
        return ref.at[:, pl.ds(pl.multiple_of(h * DIM, DIM), DIM)]

    def move(src, dst, send_sem, recv_sem, device, here, start):
        remote = pltpu.make_async_remote_copy(
            src_ref=src, dst_ref=dst, send_sem=send_sem, recv_sem=recv_sem, device_id=device, device_id_type=MESH
        )
        if start:
            @pl.when(here)
            def _():
                pltpu.make_async_copy(src, dst, recv_sem).start()

        @pl.when(jnp.logical_not(here))
        def _():
            if start:
                remote.start()
            else:
                remote.wait_send()

    def move_kv(phase, start):
        def body(j, carry):
            device, full, half, col, here = target(phase, j)
            sem = recv_in.at[row_there, col]
            for i, (ref, send) in enumerate(((k_ref, send_k), (v_ref, send_v))):
                move(part(ref, full), kv.at[1, row_there, col, 0, i, c], send.at[phase, j, 0], sem, device, here, start)

            def halves():
                for i, (ref, send) in enumerate(((k_ref, send_k), (v_ref, send_v))):
                    move(part(ref, half), kv.at[1, row_there, col, 1, i, c], send.at[phase, j, 1], sem, device, here, start)

            if phase == 0:
                halves()
            else:
                pl.when(near == 1)(halves)
            return carry

        lax.fori_loop(0, 8, body, 0)

    def move_q(phase, start):
        def body(j, carry):
            device, full, half, col, here = target(phase, j)
            move(part(q_ref, full), qb.at[col, row_there, c], send_q.at[phase, j, 0], recv_q.at[0], device, here, start)
            if phase == 0:
                move(part(q_ref, half), qb.at[4 + col, row_there, c], send_q.at[phase, j, 1], recv_q.at[0], device, here, start)
            return carry

        lax.fori_loop(0, 8, body, 0)

    def move_mask(start):
        for j in range(2):
            x_t = 2 * c + j
            here = (x_t == x) & (core_there == c)
            move(mask_ref, mb.at[row_there], send_mask.at[j], recv_mask.at[0],
                 (z * ROWS + x_t, 2 * y + core_there), here, start)

    move_kv(0, True)
    move_kv(1, True)
    move_mask(True)
    move_q(0, True)
    move_q(1, True)

    def chunk(slot, row, col):
        return kv.at[slot, row, col] if col < 3 else kv.at[slot, row, col, 0]

    def wait_for(ref, sem):
        pltpu.make_async_copy(ref, ref, sem).wait()

    def pass_on(row, col):
        return [
            pltpu.make_async_remote_copy(
                src_ref=chunk(1, row, col), dst_ref=chunk(slot, row, col),
                send_sem=send_z.at[slot // 2, row, col], recv_sem=recv_z.at[slot // 2, row, col],
                device_id=(there, head), device_id_type=MESH,
            )
            for slot, there in ((0, above), (2, below))
        ]

    def across(slot, col):
        return pltpu.make_async_remote_copy(
            src_ref=chunk(slot, 1, col), dst_ref=chunk(slot, 2, col),
            send_sem=send_x.at[slot, col], recv_sem=recv_x.at[slot, col],
            device_id=(seq, 2 * y + 1 - c), device_id_type=MESH,
        )

    for cols in ((0, 1), (2, 3)):
        for row in (1, 0):
            for col in cols:
                wait_for(chunk(1, row, col), recv_in.at[row, col])
                for copy in pass_on(row, col):
                    copy.start()
                if row == 1:
                    across(1, col).start()

    wait_for(mb, recv_mask.at[0])
    flags = mb[...]
    kept = jnp.where(flags > 0, 1.0, 0.0).astype(F32)
    forward = [kept[r, i:i + 1, :] for r in range(2) for i in range(4)]
    backward = [kept[r, 3 - i:4 - i, :] for r in range(2) for i in range(4)]
    forward, backward = jnp.concatenate(forward, axis=0), jnp.concatenate(backward, axis=0)
    kept = jnp.where(p == 0, forward, backward).astype(BF16)
    lane = lax.broadcasted_iota(jnp.int32, (256, 128), 1)
    tile = lax.broadcasted_iota(jnp.int32, (256, 128), 0)
    slot_of = jnp.where(lane >= 12, 1, 0) + jnp.where(lane >= 24, 1, 0)
    rest = lane - 12 * slot_of
    row_of, col_of = lax.shift_right_logical(rest, 2), lax.bitwise_and(rest, 3)
    row_of = jnp.where(c == 0, row_of, 3 - row_of)
    col_of = jnp.where(p == 0, col_of, 3 - col_of)
    wanted = ((z + slot_of - 1) * ROWS + row_of) * COLS + col_of
    select = jnp.where((wanted == tile) & (lane < 36), 1.0, 0.0).astype(BF16)
    picked = jnp.dot(kept, select, preferred_element_type=F32)
    offset = jnp.where(picked > 0.5, 0.0, MASKED)
    for i in range(36):
        bias[:, i * 128:(i + 1) * 128] = jnp.broadcast_to(offset[:, i:i + 1], (8, 128))

    wait_for(qb, recv_q.at[0])
    factor = math.log2(math.e) / math.sqrt(DIM)

    def attend(g, slots, first):
        hd, mid = (0, g) if g < 4 else (1, g - 4)
        lo, hi = max(0, mid - 1), min(3, mid + 1)
        n = hi - lo + 1
        blocks = [(slot, row) for slot in slots for row in range(3)]
        query = qb[g].reshape(2 * TILE, DIM)
        best = [None, None]
        for b, (slot, row) in enumerate(blocks):
            r0 = 0 if row < 2 else 1
            keys = kv[slot, row, lo:hi + 1, hd, 0].reshape(n * TILE, DIM)
            s = lax.dot_general(query[r0 * TILE:], keys, (((1,), (1,)), ((), ())), preferred_element_type=F32)
            for r in range(r0, 2):
                for t in range(n):
                    lanes = (slot * 12 + row * 4 + lo + t) * 128
                    piece = s[(r - r0) * TILE:(r - r0 + 1) * TILE, t * 128:(t + 1) * 128] * factor
                    piece = piece + bias[r * 4 + mid:r * 4 + mid + 1, lanes:lanes + 128]
                    scores[r, b * n + t] = piece
                    best[r] = piece if best[r] is None else jnp.maximum(best[r], piece)
        for r in range(2):
            highest = jnp.broadcast_to(jnp.max(best[r], axis=1, keepdims=True), (TILE, 128))
            if first:
                now, sums = highest, jnp.zeros((TILE, 128), F32)
            else:
                before = top[g, r]
                now = jnp.maximum(before, highest)
                shrink = jnp.exp2(before - now)
                sums = total[g, r] * shrink
                acc[g, r] = acc[g, r] * shrink
            for b, (slot, row) in enumerate(blocks):
                if row == 2 and r == 0:
                    continue
                for t in range(n):
                    weight = jnp.exp2(scores[r, b * n + t] - now)
                    sums = sums + weight
                    probs[r * TILE:(r + 1) * TILE, (b * n + t) * 128:(b * n + t + 1) * 128] = weight.astype(BF16)
            top[g, r], total[g, r] = now, sums
        result = [None, None]
        for b, (slot, row) in enumerate(blocks):
            r0 = 0 if row < 2 else 1
            vals = kv[slot, row, lo:hi + 1, hd, 1].reshape(n * TILE, DIM)
            o = jnp.dot(probs[r0 * TILE:, b * n * 128:(b + 1) * n * 128], vals, preferred_element_type=F32)
            for r in range(r0, 2):
                add = o[(r - r0) * TILE:(r - r0 + 1) * TILE]
                result[r] = add if result[r] is None else result[r] + add
        for r in range(2):
            acc[g, r] = result[r] if first else acc[g, r] + result[r]

    def bring(cols):
        for col in cols:
            for i, slot in enumerate((0, 2)):
                wait_for(chunk(slot, 1, col), recv_z.at[i, 1, col])
                across(slot, col).start()

    for cols, groups in (((0, 1), (0, 4)), ((2,), (1, 5)), ((3,), (2, 3))):
        for col in cols:
            wait_for(chunk(1, 2, col), recv_x.at[1, col])
        for g in groups:
            attend(g, (1,), True)
        if cols[0] > 0:
            bring((0, 1) if cols == (2,) else (2, 3))

    def send_back(g, start):
        hd, mid = (0, g) if g < 4 else (1, g - 4)
        y_t = jnp.where(p == 0, mid, 3 - mid)
        h = 3 * pair + (2 * p if hd == 0 else 1)
        for r in range(2):
            x_t = jnp.where(c == 0, r, 3 - r)
            for half in range(2):
                here = (x_t == x) & (y_t == y) & (c == half)
                move(ob.at[g, r, half], part(out_ref, h), send_out.at[g, r, half], recv_out.at[0],
                     (z * ROWS + x_t, 2 * y_t + half), here, start)

    for cols, groups in (((0, 1), (0, 4)), ((2,), (1, 5)), ((3,), (2, 3))):
        for col in cols:
            for i, slot in enumerate((0, 2)):
                wait_for(chunk(slot, 0, col), recv_z.at[i, 0, col])
                wait_for(chunk(slot, 2, col), recv_x.at[slot, col])
        for g in groups:
            attend(g, (0, 2), False)
            for r in range(2):
                whole = jnp.sum(total[g, r], axis=1, keepdims=True)
                ob[g, r] = (acc[g, r] / whole).astype(BF16).reshape(2, HALF, DIM)
            send_back(g, True)

    wait_for(out_ref, recv_out.at[0])
    move_kv(0, False)
    move_kv(1, False)
    move_mask(False)
    move_q(0, False)
    move_q(1, False)
    for col in range(4):
        for row in range(2):
            for copy in pass_on(row, col):
                copy.wait_send()
        for slot in range(3):
            across(slot, col).wait_send()
    for g in range(GROUPS):
        send_back(g, False)


def body(queries, keys, values, tile_mask):
    dma = pltpu.SemaphoreType.DMA
    return pl.pallas_call(
        kernel,
        out_shape=jax.ShapeDtypeStruct(queries.shape, BF16),
        in_specs=[pl.BlockSpec(memory_space=pl.ANY)] * 4,
        out_specs=pl.BlockSpec(memory_space=pl.ANY),
        scratch_shapes=[
            pltpu.VMEM((3, 3, 4, 2, 2, 2, HALF, DIM), BF16),
            pltpu.VMEM((GROUPS, 2, 2, HALF, DIM), BF16),
            pltpu.VMEM((2, 4, 256), jnp.int32),
            pltpu.VMEM((8, 36 * 128), F32),
            pltpu.VMEM((2, 18, TILE, 128), F32),
            pltpu.VMEM((2 * TILE, 18 * 128), BF16),
            pltpu.VMEM((GROUPS, 2, TILE, 128), F32),
            pltpu.VMEM((GROUPS, 2, TILE, 128), F32),
            pltpu.VMEM((GROUPS, 2, TILE, DIM), F32),
            pltpu.VMEM((GROUPS, 2, 2, HALF, DIM), BF16),
            dma((2, 4)), dma((2, 2, 4)), dma((3, 4)), dma((1,)), dma((1,)), dma((1,)),
            dma((2, 8, 2)), dma((2, 8, 2)), dma((2, 8, 2)), dma((2,)), dma((2, 2, 4)), dma((3, 4)), dma((GROUPS, 2, 2)),
        ],
        compiler_params=pltpu.CompilerParams(
            collective_id=0, has_side_effects=True, vmem_limit_bytes=48 * 1024 * 1024
        ),
        cost_estimate=pl.CostEstimate(flops=2_000_000_000, bytes_accessed=8_000_000, transcendentals=4_000_000),
    )(queries, keys, values, tile_mask)


def solution(mesh):
    placed = (
        P(("seq", "head"), None),
        P(("seq", "head"), None),
        P(("seq", "head"), None),
        P("seq", None),
    )
    return jax.shard_map(
        body, mesh=mesh, in_specs=placed, out_specs=P(("seq", "head"), None), check_vma=False
    )
```

time: 221 us -> 64.6 us (0.29)
  the two profiles are of different devices: /device:TPU:70 before, /device:TPU:1 now
where the time goes in v1:
time: 64.6 us; the launch traced here: 64.3 us
  Pallas kernels  59.9 us (93%)
  local copies, waits for them, and re-layouts  4.42 us (7%)
    pallas_call x1, Pallas kernels, body(): pl.pallas_call(kernel, out_shape=jax.ShapeDtypeStruct(queries.shape, BF16...  59.9 us
    unnamed x9, local copies, waits for them, and re-layouts  4.42 us

profile of v1, /device:TPU:1, one launch (start us, length us, event | category | flops | bytes accessed | tf_op | source)
XLA Modules:
  0.0 64.3 jit_solution(4561271395342229800)
XLA Ops:
  0.0 0.0 copy-start
  0.0 1.0 %copy-done = bf16[64,3072]{1,0:T(8,128)(2,1)S(1)} copy-done((bf16[64,3072]{1,0:T(8,128)(2,1)S(1)}, bf16[64,3072]{1,0:T(8,128)(2,1)}, u32[]{:S(2)}) %copy-start) | copy-done | bytes 393240
  1.0 0.0 copy-start.1
  1.0 1.0 %copy-done.1 = bf16[64,3072]{1,0:T(8,128)(2,1)S(1)} copy-done((bf16[64,3072]{1,0:T(8,128)(2,1)S(1)}, bf16[64,3072]{1,0:T(8,128)(2,1)}, u32[]{:S(2)}) %copy-start.1) | copy-done | bytes 393240
  2.0 0.0 copy-start.2
  2.0 1.0 %copy-done.2 = bf16[64,3072]{1,0:T(8,128)(2,1)S(1)} copy-done((bf16[64,3072]{1,0:T(8,128)(2,1)S(1)}, bf16[64,3072]{1,0:T(8,128)(2,1)}, u32[]{:S(2)}) %copy-start.2) | copy-done | bytes 393240
  3.0 0.0 copy-start.3
  3.0 0.7 %copy-done.3 = s32[4,256]{1,0:T(4,128)S(1)} copy-done((s32[4,256]{1,0:T(4,128)S(1)}, s32[4,256]{1,0:T(4,128)}, u32[]{:S(2)}) %copy-start.3) | copy-done | bytes 4120
  3.7 59.9 %shard_map.46 = bf16[64,3072]{1,0:T(8,128)(2,1)S(1)} custom-call(bf16[64,3072]{1,0:T(8,128)(2,1)S(1)} %copy-done, bf16[64,3072]{1,0:T(8,128)(2,1)S(1)} %copy-done.1, bf16[64,3072]{1,0:T(8,128)(2,1)S(1)} %copy-done.2, s32[4,256]{1,0:T(4,128)S(1)} %copy-done.3), custom_call_target="tpu_custom_call" | custom-call | flops 2000000000 | bytes 8000000 | tf_op jit(solution)/shard_map/pallas_call | solution.py:274
  63.6 0.7 %copy.6 = bf16[64,3072]{1,0:T(8,128)(2,1)} copy(bf16[64,3072]{1,0:T(8,128)(2,1)S(1)} %shard_map.46) | data formatting | bytes 786432
Async XLA Ops:
  0.0 1.0 %copy-start = (bf16[64,3072]{1,0:T(8,128)(2,1)S(1)}, bf16[64,3072]{1,0:T(8,128)(2,1)}, u32[]{:S(2)}) copy-start(bf16[64,3072]{1,0:T(8,128)(2,1)} %q_ref.1) | copy-start | bytes 1179652
  1.0 1.0 %copy-start.1 = (bf16[64,3072]{1,0:T(8,128)(2,1)S(1)}, bf16[64,3072]{1,0:T(8,128)(2,1)}, u32[]{:S(2)}) copy-start(bf16[64,3072]{1,0:T(8,128)(2,1)} %k_ref.1) | copy-start | bytes 1179652
  2.0 1.0 %copy-start.2 = (bf16[64,3072]{1,0:T(8,128)(2,1)S(1)}, bf16[64,3072]{1,0:T(8,128)(2,1)}, u32[]{:S(2)}) copy-start(bf16[64,3072]{1,0:T(8,128)(2,1)} %v_ref.1) | copy-start | bytes 1179652
  3.0 0.7 %copy-start.3 = (s32[4,256]{1,0:T(4,128)S(1)}, s32[4,256]{1,0:T(4,128)}, u32[]{:S(2)}) copy-start(s32[4,256]{1,0:T(4,128)} %mask_ref.1) | copy-start | bytes 12292

commit v2 on v1

--- a/solution.py
+++ b/solution.py
@@ -21,7 +21,7 @@
     seq, head = lax.axis_index("seq"), lax.axis_index("head")
     z, x = seq // ROWS, seq % ROWS
     y, c = head // 2, head % 2
-    p, pair = y % 2, 2 * x + y // 2
+    p, pair = y // 2, 2 * x + y % 2
 
     barrier = pltpu.get_barrier_semaphore()
     own = x * 8 + head
@@ -44,9 +44,9 @@
 
     def target(phase, j):
         p_t = (y // 2 + phase) % 2
-        x_t = (x + j) % 4
-        yh_t = (y // 2 + j // 4) % 2
-        y_t = 2 * yh_t + p_t
+        x_t = (x + j // 2 + 2 * near) % 4
+        yh_t = (y + c + j) % 2
+        y_t = 2 * p_t + yh_t
         w_t = 2 * x_t + yh_t
         col = near if phase == 0 else 3 - near
         here = (x_t == x) & (y_t == y) & (core_there == c)
@@ -114,7 +114,7 @@
     move_q(1, True)
 
     def chunk(slot, row, col):
-        return kv.at[slot, row, col] if col < 3 else kv.at[slot, row, col, 0]
+        return kv.at[slot, row, col, 0] if isinstance(col, int) and col == 3 else kv.at[slot, row, col]
 
     def wait_for(ref, sem):
         pltpu.make_async_copy(ref, ref, sem).wait()
@@ -136,22 +136,41 @@
             device_id=(seq, 2 * y + 1 - c), device_id_type=MESH,
         )
 
-    for cols in ((0, 1), (2, 3)):
-        for row in (1, 0):
-            for col in cols:
-                wait_for(chunk(1, row, col), recv_in.at[row, col])
-                for copy in pass_on(row, col):
-                    copy.start()
-                if row == 1:
-                    across(1, col).start()
+    def forward(row, col):
+        wait_for(chunk(1, row, col), recv_in.at[row, col])
+        for copy in pass_on(row, col):
+            copy.start()
+
+    def forward_near(i, carry):
+        gap = (x + 4 - i) % 4
+        x_from = 2 * c + gap % 2
+        col = ((gap + 4 - x_from) % 4) // 2
+        row = jnp.where(c == 0, x_from, 3 - x_from)
+        forward(row, col)
+
+        @pl.when(row == 1)
+        def _():
+            across(1, col).start()
+
+        return carry
+
+    lax.fori_loop(0, 4, forward_near, 0)
+
+    def forward_far(col):
+        forward(1, col)
+        across(1, col).start()
+        forward(0, col)
+
+    forward_far(2)
+    forward_far(3)
 
     wait_for(mb, recv_mask.at[0])
     flags = mb[...]
     kept = jnp.where(flags > 0, 1.0, 0.0).astype(F32)
-    forward = [kept[r, i:i + 1, :] for r in range(2) for i in range(4)]
-    backward = [kept[r, 3 - i:4 - i, :] for r in range(2) for i in range(4)]
-    forward, backward = jnp.concatenate(forward, axis=0), jnp.concatenate(backward, axis=0)
-    kept = jnp.where(p == 0, forward, backward).astype(BF16)
+    ahead = [kept[r, i:i + 1, :] for r in range(2) for i in range(4)]
+    back = [kept[r, 3 - i:4 - i, :] for r in range(2) for i in range(4)]
+    ahead, back = jnp.concatenate(ahead, axis=0), jnp.concatenate(back, axis=0)
+    kept = jnp.where(p == 0, ahead, back).astype(BF16)
     lane = lax.broadcasted_iota(jnp.int32, (256, 128), 1)
     tile = lax.broadcasted_iota(jnp.int32, (256, 128), 0)
     slot_of = jnp.where(lane >= 12, 1, 0) + jnp.where(lane >= 24, 1, 0)
@@ -222,13 +241,17 @@
                 wait_for(chunk(slot, 1, col), recv_z.at[i, 1, col])
                 across(slot, col).start()
 
-    for cols, groups in (((0, 1), (0, 4)), ((2,), (1, 5)), ((3,), (2, 3))):
-        for col in cols:
-            wait_for(chunk(1, 2, col), recv_x.at[1, col])
-        for g in groups:
-            attend(g, (1,), True)
-        if cols[0] > 0:
-            bring((0, 1) if cols == (2,) else (2, 3))
+    for col in (0, 1):
+        wait_for(chunk(1, 2, col), recv_x.at[1, col])
+    attend(0, (1,), True)
+    attend(4, (1,), True)
+    bring((0, 1))
+    wait_for(chunk(1, 2, 2), recv_x.at[1, 2])
+    for g in (1, 5):
+        attend(g, (1,), True)
+    wait_for(chunk(1, 2, 3), recv_x.at[1, 3])
+    for g in (2, 3):
+        attend(g, (1,), True)
 
     def send_back(g, start):
         hd, mid = (0, g) if g < 4 else (1, g - 4)
@@ -242,6 +265,8 @@
                      (z * ROWS + x_t, 2 * y_t + half), here, start)
 
     for cols, groups in (((0, 1), (0, 4)), ((2,), (1, 5)), ((3,), (2, 3))):
+        if cols[0] > 0:
+            bring(cols)
         for col in cols:
             for i, slot in enumerate((0, 2)):
                 wait_for(chunk(slot, 0, col), recv_z.at[i, 0, col])
@@ -291,7 +316,7 @@
             dma((2, 8, 2)), dma((2, 8, 2)), dma((2, 8, 2)), dma((2,)), dma((2, 2, 4)), dma((3, 4)), dma((GROUPS, 2, 2)),
         ],
         compiler_params=pltpu.CompilerParams(
-            collective_id=0, has_side_effects=True, vmem_limit_bytes=48 * 1024 * 1024
+            collective_id=0, has_side_effects=True, vmem_limit_bytes=62 * 1024 * 1024
         ),
         cost_estimate=pl.CostEstimate(flops=2_000_000_000, bytes_accessed=8_000_000, transcendentals=4_000_000),
     )(queries, keys, values, tile_mask)

time: 64.6 us -> 56.1 us (0.87)
  Pallas kernels: 59.9 us -> 54.2 us
  local copies, waits for them, and re-layouts: 4.42 us -> 1.77 us
    pallas_call x1, Pallas kernels: 59.9 us -> 54.2 us  [body(): pl.pallas_call(kernel, out_shape=jax.ShapeDtypeStruct(queries.shape, BF16...]
    unnamed x9 -> x1, local copies, waits for them, and re-layouts: 4.42 us -> 1.77 us
where the time goes in v2:
time: 56.1 us; the launch traced here: 56 us
  Pallas kernels  54.2 us (97%)
  local copies, waits for them, and re-layouts  1.77 us (3%)
    pallas_call x1, Pallas kernels, body(): pl.pallas_call(kernel, out_shape=jax.ShapeDtypeStruct(queries.shape, BF16...  54.2 us
    unnamed x1, local copies, waits for them, and re-layouts  1.77 us

profile of v2, /device:TPU:1, one launch (start us, length us, event | category | flops | bytes accessed | tf_op | source)
XLA Modules:
  0.0 56.0 jit_solution(18382562335687485082)
XLA Ops:
  0.0 54.2 %shard_map.46 = bf16[64,3072]{1,0:T(8,128)(2,1)} custom-call(bf16[64,3072]{1,0:T(8,128)(2,1)} %q_ref.1, bf16[64,3072]{1,0:T(8,128)(2,1)} %k_ref.1, bf16[64,3072]{1,0:T(8,128)(2,1)} %v_ref.1, s32[4,256]{1,0:T(4,128)} %mask_ref.1), custom_call_target="tpu_custom_call" | custom-call | flops 2000000000 | bytes 8000000 | tf_op jit(solution)/shard_map/pallas_call | solution.py:299
  54.2 1.8 %copy.6 = bf16[64,3072]{1,0:T(8,128)(2,1)} copy(bf16[64,3072]{1,0:T(8,128)(2,1)} %shard_map.46) | data formatting | bytes 786432

commit v3 on v2

--- a/solution.py
+++ b/solution.py
@@ -17,7 +17,7 @@
 
 def kernel(q_ref, k_ref, v_ref, mask_ref, out_ref, kv, qb, mb, bias, scores, probs, top, total, acc, ob,
            recv_in, recv_z, recv_x, recv_q, recv_mask, recv_out,
-           send_k, send_v, send_q, send_mask, send_z, send_x, send_out):
+           send_k, send_v, send_q, send_mask, send_z, send_x, send_out, entered):
     seq, head = lax.axis_index("seq"), lax.axis_index("head")
     z, x = seq // ROWS, seq % ROWS
     y, c = head // 2, head % 2
@@ -32,11 +32,27 @@
         return carry
 
     lax.fori_loop(1, 32, greet, 0)
-    above = ((z + 1) % FRAMES) * ROWS + x
-    below = ((z + FRAMES - 1) % FRAMES) * ROWS + x
-    for there in (above, below):
-        pl.semaphore_signal(barrier, inc=1, device_id=(there, head), device_id_type=MESH)
-    pl.semaphore_wait(barrier, 33)
+    above, below = seq + ROWS, seq - ROWS
+    has_above, has_below = z < FRAMES - 1, z > 0
+
+    @pl.when(has_above)
+    def _():
+        pl.semaphore_signal(barrier, inc=1, device_id=(above, head), device_id_type=MESH)
+
+    @pl.when(z > 1)
+    def _():
+        pl.semaphore_signal(barrier, inc=1, device_id=(below, head), device_id_type=MESH)
+
+    pl.semaphore_wait(barrier, jnp.where(z == 0, 31, jnp.where(has_above, 33, 32)))
+
+    @pl.when(z == 1)
+    def _():
+        pl.semaphore_signal(entered, inc=1, device_id=(below, head), device_id_type=MESH)
+
+    for slot, has in ((0, has_below), (2, has_above)):
+        @pl.when(jnp.logical_not(has))
+        def _():
+            kv[slot] = jnp.zeros_like(kv[slot])
 
     row_there = jnp.where(x < 2, x, 3 - x)
     core_there = x // 2
@@ -110,8 +126,6 @@
     move_kv(0, True)
     move_kv(1, True)
     move_mask(True)
-    move_q(0, True)
-    move_q(1, True)
 
     def chunk(slot, row, col):
         return kv.at[slot, row, col, 0] if isinstance(col, int) and col == 3 else kv.at[slot, row, col]
@@ -121,12 +135,12 @@
 
     def pass_on(row, col):
         return [
-            pltpu.make_async_remote_copy(
+            (has, pltpu.make_async_remote_copy(
                 src_ref=chunk(1, row, col), dst_ref=chunk(slot, row, col),
                 send_sem=send_z.at[slot // 2, row, col], recv_sem=recv_z.at[slot // 2, row, col],
                 device_id=(there, head), device_id_type=MESH,
-            )
-            for slot, there in ((0, above), (2, below))
+            ))
+            for slot, there, has in ((0, above, has_above), (2, below, has_below))
         ]
 
     def across(slot, col):
@@ -138,8 +152,8 @@
 
     def forward(row, col):
         wait_for(chunk(1, row, col), recv_in.at[row, col])
-        for copy in pass_on(row, col):
-            copy.start()
+        for has, copy in pass_on(row, col):
+            pl.when(has)(copy.start)
 
     def forward_near(i, carry):
         gap = (x + 4 - i) % 4
@@ -154,7 +168,13 @@
 
         return carry
 
+    @pl.when(z == 0)
+    def _():
+        pl.semaphore_wait(entered, 1)
+
     lax.fori_loop(0, 4, forward_near, 0)
+    move_q(0, True)
+    move_q(1, True)
 
     def forward_far(col):
         forward(1, col)
@@ -237,9 +257,11 @@
 
     def bring(cols):
         for col in cols:
-            for i, slot in enumerate((0, 2)):
-                wait_for(chunk(slot, 1, col), recv_z.at[i, 1, col])
-                across(slot, col).start()
+            for i, (slot, has) in enumerate(((0, has_below), (2, has_above))):
+                @pl.when(has)
+                def _():
+                    wait_for(chunk(slot, 1, col), recv_z.at[i, 1, col])
+                    across(slot, col).start()
 
     for col in (0, 1):
         wait_for(chunk(1, 2, col), recv_x.at[1, col])
@@ -268,9 +290,11 @@
         if cols[0] > 0:
             bring(cols)
         for col in cols:
-            for i, slot in enumerate((0, 2)):
-                wait_for(chunk(slot, 0, col), recv_z.at[i, 0, col])
-                wait_for(chunk(slot, 2, col), recv_x.at[slot, col])
+            for i, (slot, has) in enumerate(((0, has_below), (2, has_above))):
+                @pl.when(has)
+                def _():
+                    wait_for(chunk(slot, 0, col), recv_z.at[i, 0, col])
+                    wait_for(chunk(slot, 2, col), recv_x.at[slot, col])
         for g in groups:
             attend(g, (0, 2), False)
             for r in range(2):
@@ -286,10 +310,14 @@
     move_q(1, False)
     for col in range(4):
         for row in range(2):
-            for copy in pass_on(row, col):
+            for has, copy in pass_on(row, col):
+                pl.when(has)(copy.wait_send)
+        for slot, has in ((0, has_below), (1, None), (2, has_above)):
+            copy = across(slot, col)
+            if has is None:
                 copy.wait_send()
-        for slot in range(3):
-            across(slot, col).wait_send()
+            else:
+                pl.when(has)(copy.wait_send)
     for g in range(GROUPS):
         send_back(g, False)
 
@@ -314,6 +342,7 @@
             pltpu.VMEM((GROUPS, 2, 2, HALF, DIM), BF16),
             dma((2, 4)), dma((2, 2, 4)), dma((3, 4)), dma((1,)), dma((1,)), dma((1,)),
             dma((2, 8, 2)), dma((2, 8, 2)), dma((2, 8, 2)), dma((2,)), dma((2, 2, 4)), dma((3, 4)), dma((GROUPS, 2, 2)),
+            pltpu.SemaphoreType.REGULAR,
         ],
         compiler_params=pltpu.CompilerParams(
             collective_id=0, has_side_effects=True, vmem_limit_bytes=62 * 1024 * 1024

time: 56.1 us -> 50.8 us (0.906)
  Pallas kernels: 54.2 us -> 48.8 us
    pallas_call x1, Pallas kernels: 54.2 us -> 48.8 us  [body(): pl.pallas_call(kernel, out_shape=jax.ShapeDtypeStruct(queries.shape, BF16...]
where the time goes in v3:
time: 50.8 us; the launch traced here: 50.6 us
  Pallas kernels  48.8 us (96%)
  local copies, waits for them, and re-layouts  1.77 us (3%)
    pallas_call x1, Pallas kernels, body(): pl.pallas_call(kernel, out_shape=jax.ShapeDtypeStruct(queries.shape, BF16...  48.8 us
    unnamed x1, local copies, waits for them, and re-layouts  1.77 us

profile of v3, /device:TPU:1, one launch (start us, length us, event | category | flops | bytes accessed | tf_op | source)
XLA Modules:
  0.0 50.6 jit_solution(5934476101119556874)
XLA Ops:
  0.0 48.8 %shard_map.46 = bf16[64,3072]{1,0:T(8,128)(2,1)} custom-call(bf16[64,3072]{1,0:T(8,128)(2,1)} %q_ref.1, bf16[64,3072]{1,0:T(8,128)(2,1)} %k_ref.1, bf16[64,3072]{1,0:T(8,128)(2,1)} %v_ref.1, s32[4,256]{1,0:T(4,128)} %mask_ref.1), custom_call_target="tpu_custom_call" | custom-call | flops 2000000000 | bytes 8000000 | tf_op jit(solution)/shard_map/pallas_call | solution.py:327
  48.9 1.8 %copy.6 = bf16[64,3072]{1,0:T(8,128)(2,1)} copy(bf16[64,3072]{1,0:T(8,128)(2,1)} %shard_map.46) | data formatting | bytes 786432

commit v4 on v3

--- a/solution.py
+++ b/solution.py
@@ -13,11 +13,13 @@
 TILE, HALF, DIM = 128, 64, 128
 GROUPS = 6
 MASKED = -1e30
+PLACE = (0, 1, 4, 5, 2, 3)
 
 
 def kernel(q_ref, k_ref, v_ref, mask_ref, out_ref, kv, qb, mb, bias, scores, probs, top, total, acc, ob,
            recv_in, recv_z, recv_x, recv_q, recv_mask, recv_out,
-           send_k, send_v, send_q, send_mask, send_z, send_x, send_out, entered):
+           send_near, send_far, send_mask, send_z, send_x, send_out, entered,
+           recv_lent, send_lent, recv_lent_x):
     seq, head = lax.axis_index("seq"), lax.axis_index("head")
     z, x = seq // ROWS, seq % ROWS
     y, c = head // 2, head % 2
@@ -65,79 +67,79 @@
         y_t = 2 * p_t + yh_t
         w_t = 2 * x_t + yh_t
         col = near if phase == 0 else 3 - near
-        here = (x_t == x) & (y_t == y) & (core_there == c)
+        here = (x_t == x) & (y_t == y) & (core_there == c) if phase == 0 else None
         return (z * ROWS + x_t, 2 * y_t + core_there), 3 * w_t + 2 * p_t, 3 * w_t + 1, col, here
 
     def part(ref, h):
         return ref.at[:, pl.ds(pl.multiple_of(h * DIM, DIM), DIM)]
 
-    def move(src, dst, send_sem, recv_sem, device, here, start):
+    def wait_for(ref, sem):
+        pltpu.make_async_copy(ref, ref, sem).wait()
+
+    def move(src, dst, send_sem, recv_sem, device, here=None):
         remote = pltpu.make_async_remote_copy(
             src_ref=src, dst_ref=dst, send_sem=send_sem, recv_sem=recv_sem, device_id=device, device_id_type=MESH
         )
-        if start:
-            @pl.when(here)
-            def _():
-                pltpu.make_async_copy(src, dst, recv_sem).start()
-
-        @pl.when(jnp.logical_not(here))
-        def _():
-            if start:
-                remote.start()
-            else:
-                remote.wait_send()
-
-    def move_kv(phase, start):
+        if here is None:
+            remote.start()
+        else:
+            pl.when(here)(pltpu.make_async_copy(src, dst, recv_sem).start)
+            pl.when(jnp.logical_not(here))(remote.start)
+
+    def move_kv(phase):
         def body(j, carry):
             device, full, half, col, here = target(phase, j)
-            sem = recv_in.at[row_there, col]
-            for i, (ref, send) in enumerate(((k_ref, send_k), (v_ref, send_v))):
-                move(part(ref, full), kv.at[1, row_there, col, 0, i, c], send.at[phase, j, 0], sem, device, here, start)
-
-            def halves():
-                for i, (ref, send) in enumerate(((k_ref, send_k), (v_ref, send_v))):
-                    move(part(ref, half), kv.at[1, row_there, col, 1, i, c], send.at[phase, j, 1], sem, device, here, start)
-
+            sems = (send_near.at[j] if phase == 0 else send_far.at[0], recv_in.at[row_there, col])
+            for i, ref in enumerate((k_ref, v_ref)):
+                move(part(ref, full), kv.at[1, row_there, col, 0, i, c], *sems, device, here)
             if phase == 0:
-                halves()
-            else:
-                pl.when(near == 1)(halves)
+                for i, ref in enumerate((k_ref, v_ref)):
+                    move(part(ref, half), kv.at[1, row_there, col, 1, i, c], *sems, device, here)
             return carry
 
         lax.fori_loop(0, 8, body, 0)
 
-    def move_q(phase, start):
+    def move_q(phase):
         def body(j, carry):
             device, full, half, col, here = target(phase, j)
-            move(part(q_ref, full), qb.at[col, row_there, c], send_q.at[phase, j, 0], recv_q.at[0], device, here, start)
+            sems = (send_near.at[j] if phase == 0 else send_far.at[0], recv_q.at[phase])
+            move(part(q_ref, full), qb.at[col + 2 * phase, row_there, c], *sems, device, here)
             if phase == 0:
-                move(part(q_ref, half), qb.at[4 + col, row_there, c], send_q.at[phase, j, 1], recv_q.at[0], device, here, start)
+                move(part(q_ref, half), qb.at[2 + col, row_there, c], *sems, device, here)
             return carry
 
         lax.fori_loop(0, 8, body, 0)
 
-    def move_mask(start):
+    def sent():
+        def body(j, carry):
+            pl.when(jnp.logical_not(target(0, j)[4]))(lambda: wait_for(qb.at[pl.ds(0, 3), 0], send_near.at[j]))
+            return carry
+
+        lax.fori_loop(0, 8, body, 0)
+        wait_for(qb, send_far.at[0])
+
+    def mask_to(j):
+        x_t = 2 * c + j
+        return (z * ROWS + x_t, 2 * y + core_there), (x_t == x) & (core_there == c)
+
+    def move_mask():
         for j in range(2):
-            x_t = 2 * c + j
-            here = (x_t == x) & (core_there == c)
-            move(mask_ref, mb.at[row_there], send_mask.at[j], recv_mask.at[0],
-                 (z * ROWS + x_t, 2 * y + core_there), here, start)
-
-    move_kv(0, True)
-    move_kv(1, True)
-    move_mask(True)
+            device, here = mask_to(j)
+            move(mask_ref, mb.at[row_there], send_mask.at[j], recv_mask.at[0], device, here)
+
+    move_kv(0)
+    move_kv(1)
+    move_mask()
+    move_q(0)
 
     def chunk(slot, row, col):
-        return kv.at[slot, row, col, 0] if isinstance(col, int) and col == 3 else kv.at[slot, row, col]
-
-    def wait_for(ref, sem):
-        pltpu.make_async_copy(ref, ref, sem).wait()
+        return kv.at[slot, row, col, 0] if isinstance(col, int) and col >= 2 else kv.at[slot, row, col]
 
     def pass_on(row, col):
         return [
             (has, pltpu.make_async_remote_copy(
                 src_ref=chunk(1, row, col), dst_ref=chunk(slot, row, col),
-                send_sem=send_z.at[slot // 2, row, col], recv_sem=recv_z.at[slot // 2, row, col],
+                send_sem=send_z.at[slot // 2], recv_sem=recv_z.at[slot // 2, row, col],
                 device_id=(there, head), device_id_type=MESH,
             ))
             for slot, there, has in ((0, above, has_above), (2, below, has_below))
@@ -146,9 +148,27 @@
     def across(slot, col):
         return pltpu.make_async_remote_copy(
             src_ref=chunk(slot, 1, col), dst_ref=chunk(slot, 2, col),
-            send_sem=send_x.at[slot, col], recv_sem=recv_x.at[slot, col],
+            send_sem=send_x.at[slot], recv_sem=recv_x.at[slot, col],
             device_id=(seq, 2 * y + 1 - c), device_id_type=MESH,
         )
+
+    def lend(slot):
+        return pltpu.make_async_remote_copy(
+            src_ref=kv.at[slot, pl.ds(0, 2), 1, 1], dst_ref=kv.at[slot, pl.ds(0, 2), 2, 1],
+            send_sem=send_lent.at[slot], recv_sem=recv_lent.at[slot],
+            device_id=(seq, (head + 4) % 8), device_id_type=MESH,
+        )
+
+    def lend_across(slot):
+        return pltpu.make_async_remote_copy(
+            src_ref=kv.at[slot, 1, 2, 1], dst_ref=kv.at[slot, 2, 2, 1],
+            send_sem=send_lent.at[slot], recv_sem=recv_lent_x.at[slot],
+            device_id=(seq, 2 * y + 1 - c), device_id_type=MESH,
+        )
+
+    def borrow(slot):
+        wait_for(kv.at[slot, pl.ds(0, 2), 2, 1], recv_lent.at[slot])
+        lend_across(slot).start()
 
     def forward(row, col):
         wait_for(chunk(1, row, col), recv_in.at[row, col])
@@ -173,8 +193,8 @@
         pl.semaphore_wait(entered, 1)
 
     lax.fori_loop(0, 4, forward_near, 0)
-    move_q(0, True)
-    move_q(1, True)
+    lend(1).start()
+    move_q(1)
 
     def forward_far(col):
         forward(1, col)
@@ -205,7 +225,7 @@
     for i in range(36):
         bias[:, i * 128:(i + 1) * 128] = jnp.broadcast_to(offset[:, i:i + 1], (8, 128))
 
-    wait_for(qb, recv_q.at[0])
+    wait_for(qb.at[pl.ds(0, 4)], recv_q.at[0])
     factor = math.log2(math.e) / math.sqrt(DIM)
 
     def attend(g, slots, first):
@@ -213,7 +233,7 @@
         lo, hi = max(0, mid - 1), min(3, mid + 1)
         n = hi - lo + 1
         blocks = [(slot, row) for slot in slots for row in range(3)]
-        query = qb[g].reshape(2 * TILE, DIM)
+        query = qb[PLACE[g]].reshape(2 * TILE, DIM)
         best = [None, None]
         for b, (slot, row) in enumerate(blocks):
             r0 = 0 if row < 2 else 1
@@ -263,63 +283,100 @@
                     wait_for(chunk(slot, 1, col), recv_z.at[i, 1, col])
                     across(slot, col).start()
 
+    sides = ((0, 0, has_below), (1, 2, has_above))
+
+    def on_sides(act):
+        for i, slot, has in sides:
+            pl.when(has)(lambda: act(i, slot))
+
+    def join(cols):
+        def act(i, slot):
+            for col in cols:
+                wait_for(chunk(slot, 0, col), recv_z.at[i, 0, col])
+                wait_for(chunk(slot, 2, col), recv_x.at[slot, col])
+
+        on_sides(act)
+
+    def lend_sides(i, slot):
+        wait_for(chunk(slot, 0, 1), recv_z.at[i, 0, 1])
+        lend(slot).start()
+
     for col in (0, 1):
         wait_for(chunk(1, 2, col), recv_x.at[1, col])
     attend(0, (1,), True)
     attend(4, (1,), True)
     bring((0, 1))
+    on_sides(lend_sides)
+    borrow(1)
     wait_for(chunk(1, 2, 2), recv_x.at[1, 2])
-    for g in (1, 5):
-        attend(g, (1,), True)
+    attend(1, (1,), True)
     wait_for(chunk(1, 2, 3), recv_x.at[1, 3])
-    for g in (2, 3):
-        attend(g, (1,), True)
-
-    def send_back(g, start):
-        hd, mid = (0, g) if g < 4 else (1, g - 4)
+    wait_for(qb.at[pl.ds(4, 2)], recv_q.at[1])
+    attend(2, (1,), True)
+    attend(3, (1,), True)
+    wait_for(kv.at[1, 2, 2, 1], recv_lent_x.at[1])
+    attend(5, (1,), True)
+
+    def home(g, r):
+        mid = g if g < 4 else g - 4
+        x_t = jnp.where(c == 0, r, 3 - r)
         y_t = jnp.where(p == 0, mid, 3 - mid)
-        h = 3 * pair + (2 * p if hd == 0 else 1)
+        return x_t, y_t, (x_t == x) & (y_t == y)
+
+    def send_back(g):
+        h = 3 * pair + (2 * p if g < 4 else 1)
         for r in range(2):
-            x_t = jnp.where(c == 0, r, 3 - r)
+            x_t, y_t, mine = home(g, r)
+            sem = send_out.at[8] if g in (2, 3) else send_out.at[2 * PLACE[g] + r]
             for half in range(2):
-                here = (x_t == x) & (y_t == y) & (c == half)
-                move(ob.at[g, r, half], part(out_ref, h), send_out.at[g, r, half], recv_out.at[0],
-                     (z * ROWS + x_t, 2 * y_t + half), here, start)
-
-    for cols, groups in (((0, 1), (0, 4)), ((2,), (1, 5)), ((3,), (2, 3))):
-        if cols[0] > 0:
-            bring(cols)
-        for col in cols:
-            for i, (slot, has) in enumerate(((0, has_below), (2, has_above))):
-                @pl.when(has)
-                def _():
-                    wait_for(chunk(slot, 0, col), recv_z.at[i, 0, col])
-                    wait_for(chunk(slot, 2, col), recv_x.at[slot, col])
-        for g in groups:
-            attend(g, (0, 2), False)
-            for r in range(2):
-                whole = jnp.sum(total[g, r], axis=1, keepdims=True)
-                ob[g, r] = (acc[g, r] / whole).astype(BF16).reshape(2, HALF, DIM)
-            send_back(g, True)
-
+                move(ob.at[g, r, half], part(out_ref, h), sem, recv_out.at[0],
+                     (z * ROWS + x_t, 2 * y_t + half), None if g in (2, 3) else mine & (c == half))
+
+    def finish(g):
+        attend(g, (0, 2), False)
+        for r in range(2):
+            whole = jnp.sum(total[g, r], axis=1, keepdims=True)
+            ob[g, r] = (acc[g, r] / whole).astype(BF16).reshape(2, HALF, DIM)
+        send_back(g)
+
+    on_sides(lambda i, slot: (
+        wait_for(chunk(slot, 0, 0), recv_z.at[i, 0, 0]),
+        [wait_for(chunk(slot, 2, col), recv_x.at[slot, col]) for col in (0, 1)],
+    ) and None)
+    finish(0)
+    bring((2,))
+    finish(4)
+    join((2,))
+    finish(1)
+    bring((3,))
+    on_sides(lambda i, slot: borrow(slot))
+    join((3,))
+    finish(2)
+    finish(3)
+    on_sides(lambda i, slot: wait_for(kv.at[slot, 2, 2, 1], recv_lent_x.at[slot]))
+    finish(5)
+
+    sent()
+    for j in range(2):
+        device, here = mask_to(j)
+        pl.when(jnp.logical_not(here))(lambda: wait_for(mask_ref, send_mask.at[j]))
+    wait_for(kv.at[1, 0, pl.ds(0, 3)], send_x.at[1])
+    wait_for(kv.at[1, pl.ds(0, 3), 0, 0], send_lent.at[1])
+
+    def sides_sent(i, slot):
+        wait_for(kv.at[slot, 0, pl.ds(0, 3)], send_x.at[slot])
+        wait_for(kv.at[slot, pl.ds(0, 3), 0, 0], send_lent.at[slot])
+        wait_for(kv.at[slot, pl.ds(0, 2), pl.ds(0, 3)], send_z.at[1 - i])
+
+    on_sides(sides_sent)
+    for g in (0, 1, 4, 5):
+        for r in range(2):
+            x_t, y_t, mine = home(g, r)
+            sem = send_out.at[2 * PLACE[g] + r]
+            pl.when(mine)(lambda: wait_for(ob.at[g, r, 0], sem))
+            pl.when(jnp.logical_not(mine))(lambda: wait_for(ob.at[g, r], sem))
+    wait_for(ob.at[pl.ds(2, 2)], send_out.at[8])
     wait_for(out_ref, recv_out.at[0])
-    move_kv(0, False)
-    move_kv(1, False)
-    move_mask(False)
-    move_q(0, False)
-    move_q(1, False)
-    for col in range(4):
-        for row in range(2):
-            for has, copy in pass_on(row, col):
-                pl.when(has)(copy.wait_send)
-        for slot, has in ((0, has_below), (1, None), (2, has_above)):
-            copy = across(slot, col)
-            if has is None:
-                copy.wait_send()
-            else:
-                pl.when(has)(copy.wait_send)
-    for g in range(GROUPS):
-        send_back(g, False)
 
 
 def body(queries, keys, values, tile_mask):
@@ -340,9 +397,10 @@
             pltpu.VMEM((GROUPS, 2, TILE, 128), F32),
             pltpu.VMEM((GROUPS, 2, TILE, DIM), F32),
             pltpu.VMEM((GROUPS, 2, 2, HALF, DIM), BF16),
-            dma((2, 4)), dma((2, 2, 4)), dma((3, 4)), dma((1,)), dma((1,)), dma((1,)),
-            dma((2, 8, 2)), dma((2, 8, 2)), dma((2, 8, 2)), dma((2,)), dma((2, 2, 4)), dma((3, 4)), dma((GROUPS, 2, 2)),
+            dma((2, 4)), dma((2, 2, 4)), dma((3, 4)), dma((2,)), dma((1,)), dma((1,)),
+            dma((8,)), dma((1,)), dma((2,)), dma((2,)), dma((3,)), dma((9,)),
             pltpu.SemaphoreType.REGULAR,
+            dma((3,)), dma((3,)), dma((3,)),
         ],
         compiler_params=pltpu.CompilerParams(
             collective_id=0, has_side_effects=True, vmem_limit_bytes=62 * 1024 * 1024

time: 50.8 us -> 46.5 us (0.915)
  Pallas kernels: 48.8 us -> 44.1 us
    pallas_call x1, Pallas kernels: 48.8 us -> 44.1 us  [body(): pl.pallas_call(kernel, out_shape=jax.ShapeDtypeStruct(queries.shape, BF16...]
where the time goes in v4:
time: 46.5 us; the launch traced here: 45.8 us
  Pallas kernels  44.1 us (95%)
  local copies, waits for them, and re-layouts  1.77 us (4%)
    pallas_call x1, Pallas kernels, body(): pl.pallas_call(kernel, out_shape=jax.ShapeDtypeStruct(queries.shape, BF16...  44.1 us
    unnamed x1, local copies, waits for them, and re-layouts  1.77 us

profile of v4, /device:TPU:1, one launch (start us, length us, event | category | flops | bytes accessed | tf_op | source)
XLA Modules:
  0.0 45.8 jit_solution(10639225111898455914)
XLA Ops:
  0.0 44.1 %shard_map.46 = bf16[64,3072]{1,0:T(8,128)(2,1)} custom-call(bf16[64,3072]{1,0:T(8,128)(2,1)} %q_ref.1, bf16[64,3072]{1,0:T(8,128)(2,1)} %k_ref.1, bf16[64,3072]{1,0:T(8,128)(2,1)} %v_ref.1, s32[4,256]{1,0:T(4,128)} %mask_ref.1), custom_call_target="tpu_custom_call" | custom-call | flops 2000000000 | bytes 8000000 | tf_op jit(solution)/shard_map/pallas_call | solution.py:384
  44.1 1.8 %copy.6 = bf16[64,3072]{1,0:T(8,128)(2,1)} copy(bf16[64,3072]{1,0:T(8,128)(2,1)} %shard_map.46) | data formatting | bytes 786432

commit v5 on v4

--- a/solution.py
+++ b/solution.py
@@ -16,7 +16,7 @@
 PLACE = (0, 1, 4, 5, 2, 3)
 
 
-def kernel(q_ref, k_ref, v_ref, mask_ref, out_ref, kv, qb, mb, bias, scores, probs, top, total, acc, ob,
+def kernel(q_ref, k_ref, v_ref, mask_ref, out_ref, kv, qb, mb, bias, scores, peak, probs, top, total, acc, ob,
            recv_in, recv_z, recv_x, recv_q, recv_mask, recv_out,
            send_near, send_far, send_mask, send_z, send_x, send_out, entered,
            recv_lent, send_lent, recv_lent_x):
@@ -228,11 +228,13 @@
     wait_for(qb.at[pl.ds(0, 4)], recv_q.at[0])
     factor = math.log2(math.e) / math.sqrt(DIM)
 
-    def attend(g, slots, first):
+    def layout(g, slots):
         hd, mid = (0, g) if g < 4 else (1, g - 4)
         lo, hi = max(0, mid - 1), min(3, mid + 1)
-        n = hi - lo + 1
-        blocks = [(slot, row) for slot in slots for row in range(3)]
+        return hd, mid, lo, hi, hi - lo + 1, [(slot, row) for slot in slots for row in range(3)]
+
+    def score(g, slots, side):
+        hd, mid, lo, hi, n, blocks = layout(g, slots)
         query = qb[PLACE[g]].reshape(2 * TILE, DIM)
         best = [None, None]
         for b, (slot, row) in enumerate(blocks):
@@ -244,36 +246,51 @@
                     lanes = (slot * 12 + row * 4 + lo + t) * 128
                     piece = s[(r - r0) * TILE:(r - r0 + 1) * TILE, t * 128:(t + 1) * 128] * factor
                     piece = piece + bias[r * 4 + mid:r * 4 + mid + 1, lanes:lanes + 128]
-                    scores[r, b * n + t] = piece
+                    scores[side, r, b * n + t] = piece
                     best[r] = piece if best[r] is None else jnp.maximum(best[r], piece)
-        for r in range(2):
-            highest = jnp.broadcast_to(jnp.max(best[r], axis=1, keepdims=True), (TILE, 128))
+            yield
+        for r in range(2):
+            peak[side, r] = jnp.broadcast_to(jnp.max(best[r], axis=1, keepdims=True), (TILE, 128))
+        yield
+
+    def weigh(g, slots, side, first):
+        hd, mid, lo, hi, n, blocks = layout(g, slots)
+        now, sums, result = [None, None], [None, None], [None, None]
+        for r in range(2):
+            now[r] = peak[side, r]
             if first:
-                now, sums = highest, jnp.zeros((TILE, 128), F32)
+                sums[r] = jnp.zeros((TILE, 128), F32)
             else:
                 before = top[g, r]
-                now = jnp.maximum(before, highest)
-                shrink = jnp.exp2(before - now)
-                sums = total[g, r] * shrink
+                now[r] = jnp.maximum(before, now[r])
+                shrink = jnp.exp2(before - now[r])
+                sums[r] = total[g, r] * shrink
                 acc[g, r] = acc[g, r] * shrink
-            for b, (slot, row) in enumerate(blocks):
-                if row == 2 and r == 0:
-                    continue
-                for t in range(n):
-                    weight = jnp.exp2(scores[r, b * n + t] - now)
-                    sums = sums + weight
-                    probs[r * TILE:(r + 1) * TILE, (b * n + t) * 128:(b * n + t + 1) * 128] = weight.astype(BF16)
-            top[g, r], total[g, r] = now, sums
-        result = [None, None]
+            top[g, r] = now[r]
         for b, (slot, row) in enumerate(blocks):
             r0 = 0 if row < 2 else 1
+            for r in range(r0, 2):
+                for t in range(n):
+                    weight = jnp.exp2(scores[side, r, b * n + t] - now[r])
+                    sums[r] = sums[r] + weight
+                    probs[r * TILE:(r + 1) * TILE, (b * n + t) * 128:(b * n + t + 1) * 128] = weight.astype(BF16)
             vals = kv[slot, row, lo:hi + 1, hd, 1].reshape(n * TILE, DIM)
             o = jnp.dot(probs[r0 * TILE:, b * n * 128:(b + 1) * n * 128], vals, preferred_element_type=F32)
             for r in range(r0, 2):
                 add = o[(r - r0) * TILE:(r - r0 + 1) * TILE]
                 result[r] = add if result[r] is None else result[r] + add
-        for r in range(2):
+            yield
+        for r in range(2):
+            total[g, r] = sums[r]
             acc[g, r] = result[r] if first else acc[g, r] + result[r]
+        yield
+
+    def together(*parts):
+        parts = list(parts)
+        while parts:
+            for part_ in list(parts):
+                if next(part_, StopIteration) is StopIteration:
+                    parts.remove(part_)
 
     def bring(cols):
         for col in cols:
@@ -301,22 +318,6 @@
         wait_for(chunk(slot, 0, 1), recv_z.at[i, 0, 1])
         lend(slot).start()
 
-    for col in (0, 1):
-        wait_for(chunk(1, 2, col), recv_x.at[1, col])
-    attend(0, (1,), True)
-    attend(4, (1,), True)
-    bring((0, 1))
-    on_sides(lend_sides)
-    borrow(1)
-    wait_for(chunk(1, 2, 2), recv_x.at[1, 2])
-    attend(1, (1,), True)
-    wait_for(chunk(1, 2, 3), recv_x.at[1, 3])
-    wait_for(qb.at[pl.ds(4, 2)], recv_q.at[1])
-    attend(2, (1,), True)
-    attend(3, (1,), True)
-    wait_for(kv.at[1, 2, 2, 1], recv_lent_x.at[1])
-    attend(5, (1,), True)
-
     def home(g, r):
         mid = g if g < 4 else g - 4
         x_t = jnp.where(c == 0, r, 3 - r)
@@ -333,28 +334,57 @@
                      (z * ROWS + x_t, 2 * y_t + half), None if g in (2, 3) else mine & (c == half))
 
     def finish(g):
-        attend(g, (0, 2), False)
         for r in range(2):
             whole = jnp.sum(total[g, r], axis=1, keepdims=True)
             ob[g, r] = (acc[g, r] / whole).astype(BF16).reshape(2, HALF, DIM)
         send_back(g)
 
-    on_sides(lambda i, slot: (
-        wait_for(chunk(slot, 0, 0), recv_z.at[i, 0, 0]),
-        [wait_for(chunk(slot, 2, col), recv_x.at[slot, col]) for col in (0, 1)],
-    ) and None)
-    finish(0)
-    bring((2,))
-    finish(4)
-    join((2,))
-    finish(1)
-    bring((3,))
-    on_sides(lambda i, slot: borrow(slot))
-    join((3,))
-    finish(2)
-    finish(3)
-    on_sides(lambda i, slot: wait_for(kv.at[slot, 2, 2, 1], recv_lent_x.at[slot]))
-    finish(5)
+    def before_own(g):
+        if g == 0:
+            for col in (0, 1):
+                wait_for(chunk(1, 2, col), recv_x.at[1, col])
+        if g == 1:
+            wait_for(chunk(1, 2, 2), recv_x.at[1, 2])
+        if g == 2:
+            bring((1,))
+            on_sides(lend_sides)
+            bring((0,))
+            borrow(1)
+            wait_for(chunk(1, 2, 3), recv_x.at[1, 3])
+            wait_for(qb.at[pl.ds(4, 2)], recv_q.at[1])
+        if g == 5:
+            wait_for(kv.at[1, 2, 2, 1], recv_lent_x.at[1])
+
+    def before_sides(g):
+        if g == 0:
+            on_sides(lambda i, slot: (
+                wait_for(chunk(slot, 0, 0), recv_z.at[i, 0, 0]),
+                [wait_for(chunk(slot, 2, col), recv_x.at[slot, col]) for col in (0, 1)],
+            ) and None)
+        if g == 4:
+            bring((2,))
+        if g == 1:
+            join((2,))
+        if g == 2:
+            bring((3,))
+            join((3,))
+        if g == 5:
+            on_sides(lambda i, slot: borrow(slot))
+            on_sides(lambda i, slot: wait_for(kv.at[slot, 2, 2, 1], recv_lent_x.at[slot]))
+
+    jobs = [(g, (1,), True) for g in (0, 4, 1, 2, 3, 5)] + [(g, (0, 2), False) for g in (0, 4, 1, 2, 3, 5)]
+    old = None
+    for i, (g, slots, first) in enumerate(jobs + [(None, None, None)]):
+        now_running = []
+        if g is not None:
+            (before_own if first else before_sides)(g)
+            now_running.append(score(g, slots, i % 2))
+        if old:
+            now_running.append(weigh(*old))
+        together(*now_running)
+        if old and not old[3]:
+            finish(old[0])
+        old = (g, slots, i % 2, first)
 
     sent()
     for j in range(2):
@@ -391,7 +421,8 @@
             pltpu.VMEM((GROUPS, 2, 2, HALF, DIM), BF16),
             pltpu.VMEM((2, 4, 256), jnp.int32),
             pltpu.VMEM((8, 36 * 128), F32),
-            pltpu.VMEM((2, 18, TILE, 128), F32),
+            pltpu.VMEM((2, 2, 18, TILE, 128), F32),
+            pltpu.VMEM((2, 2, TILE, 128), F32),
             pltpu.VMEM((2 * TILE, 18 * 128), BF16),
             pltpu.VMEM((GROUPS, 2, TILE, 128), F32),
             pltpu.VMEM((GROUPS, 2, TILE, 128), F32),

time: 46.5 us -> 46.4 us (level)
  no operation moved by 1% of the time
where the time goes in v5:
time: 46.4 us; the launch traced here: 45.6 us
  Pallas kernels  43.8 us (94%)
  local copies, waits for them, and re-layouts  1.77 us (4%)
    pallas_call x1, Pallas kernels, body(): pl.pallas_call(kernel, out_shape=jax.ShapeDtypeStruct(queries.shape, BF16...  43.8 us
    unnamed x1, local copies, waits for them, and re-layouts  1.77 us

profile of v5, /device:TPU:1, one launch (start us, length us, event | category | flops | bytes accessed | tf_op | source)
XLA Modules:
  0.0 45.6 jit_solution(3508979232931891078)
XLA Ops:
  0.0 43.8 %shard_map.46 = bf16[64,3072]{1,0:T(8,128)(2,1)} custom-call(bf16[64,3072]{1,0:T(8,128)(2,1)} %q_ref.1, bf16[64,3072]{1,0:T(8,128)(2,1)} %k_ref.1, bf16[64,3072]{1,0:T(8,128)(2,1)} %v_ref.1, s32[4,256]{1,0:T(4,128)} %mask_ref.1), custom_call_target="tpu_custom_call" | custom-call | flops 2000000000 | bytes 8000000 | tf_op jit(solution)/shard_map/pallas_call | solution.py:414
  43.8 1.8 %copy.6 = bf16[64,3072]{1,0:T(8,128)(2,1)} copy(bf16[64,3072]{1,0:T(8,128)(2,1)} %shard_map.46) | data formatting | bytes 786432

commit v6 on v5

--- a/solution.py
+++ b/solution.py
@@ -29,8 +29,8 @@
     own = x * 8 + head
 
     def greet(k, carry):
-        other = (own + k) % 32
-        pl.semaphore_signal(barrier, inc=1, device_id=(z * ROWS + other // 8, other % 8), device_id_type=MESH)
+        other = lax.bitwise_and(own + k, 31)
+        pl.semaphore_signal(barrier, inc=1, device_id=(seq - x + lax.shift_right_logical(other, 3), lax.bitwise_and(other, 7)), device_id_type=MESH)
         return carry
 
     lax.fori_loop(1, 32, greet, 0)
@@ -376,6 +376,10 @@
     old = None
     for i, (g, slots, first) in enumerate(jobs + [(None, None, None)]):
         now_running = []
+        if g == 5 and not first:
+            together(weigh(*old))
+            finish(old[0])
+            old = None
         if g is not None:
             (before_own if first else before_sides)(g)
             now_running.append(score(g, slots, i % 2))

time: 46.4 us -> 45.7 us (0.985); the launches traced: 45.6 us -> 45.5 us
  no operation moved by 1% of the time
where the time goes in v6:
time: 45.7 us; the launch traced here: 45.5 us
  Pallas kernels  43.7 us (96%)
  local copies, waits for them, and re-layouts  1.77 us (4%)
    pallas_call x1, Pallas kernels, body(): pl.pallas_call(kernel, out_shape=jax.ShapeDtypeStruct(queries.shape, BF16...  43.7 us
    unnamed x1, local copies, waits for them, and re-layouts  1.77 us

profile of v6, /device:TPU:1, one launch (start us, length us, event | category | flops | bytes accessed | tf_op | source)
XLA Modules:
  0.0 45.5 jit_solution(17580972875211226524)
XLA Ops:
  0.0 43.7 %shard_map.46 = bf16[64,3072]{1,0:T(8,128)(2,1)} custom-call(bf16[64,3072]{1,0:T(8,128)(2,1)} %q_ref.1, bf16[64,3072]{1,0:T(8,128)(2,1)} %k_ref.1, bf16[64,3072]{1,0:T(8,128)(2,1)} %v_ref.1, s32[4,256]{1,0:T(4,128)} %mask_ref.1), custom_call_target="tpu_custom_call" | custom-call | flops 2000000000 | bytes 8000000 | tf_op jit(solution)/shard_map/pallas_call | solution.py:418
  43.7 1.8 %copy.6 = bf16[64,3072]{1,0:T(8,128)(2,1)} copy(bf16[64,3072]{1,0:T(8,128)(2,1)} %shard_map.46) | data formatting | bytes 786432
